TPU v7x, 32 devices: a whole 2x2x4 slice. The times are simulated.
32 devices in a mesh: section: 4 (over z), seq: 8 (over y, x, core).
Axes of the slice: x: 2, y: 2, z: 4, core: 2. Of those that a mesh axis runs over, the one named last changes fastest.
Arguments:
- projected: bfloat16 [4, 3, 4096, 3072], P('section', None, 'seq'), may hold values from -24 to 24
- gate: bfloat16 [4, 3072], P('section'), may hold values from 2 to 8
- head_class: int32 [24], replicated, may hold values 0 or 1
- tile_lists: int32 [2, 32, 8], replicated, may hold values from 0 to 31, as said below
- tile_counts: int32 [24, 32], replicated, may hold values from 1 to 8, as said below
Outputs:
- next_input: bfloat16 [4, 4096, 3072], P('section', 'seq')
Inputs may be any that keep to these rules, and one draw needn't show every extreme that they name: tile_lists[c, t, 0] = t, and the 8 entries of a row are distinct tiles. `tile_counts`: counts differ strongly from head to head.
All inputs are finite; a program needn't handle non-finite values.
Results may differ from a plain program's by a relative error of at most 0.0057.
Values may be sent and summed in bfloat16 or wider, within the bound.
A program may use at most 128 MiB of HBM per device.

v0:
```python
import jax
import jax.numpy as jnp
from jax import lax
from jax.sharding import PartitionSpec as P

H = 24
HD = 128
QG = 8


def from_behind(block, axis, distance):
    devices = range(lax.axis_size(axis))
    route = [((i - distance) % len(devices), i) for i in devices]
    return lax.ppermute(block, axis, route)


def attend_tiles(query_tiles, key_tiles, value_tiles, tile_rows, counts):
    ntiles = tile_rows.shape[0]
    kmax = tile_rows.shape[1]
    tile_len = query_tiles.shape[1]
    depth = query_tiles.shape[2]
    scale_factor = depth ** (-0.5)

    def one_group(group):
        offset = group * QG
        group_queries = lax.dynamic_slice_in_dim(query_tiles, offset, QG, 0)
        group_rows = lax.dynamic_slice_in_dim(tile_rows, offset, QG, 0)
        group_counts = lax.dynamic_slice_in_dim(counts, offset, QG, 0)
        gathered_keys = key_tiles[group_rows].reshape(QG, kmax * tile_len, depth)
        gathered_values = value_tiles[group_rows].reshape(QG, kmax * tile_len, depth)
        scores = (
            jnp.einsum(
                "qtd,qkd->qtk", group_queries, gathered_keys, preferred_element_type=jnp.float32
            )
            * scale_factor
        )
        usable = jnp.arange(kmax, dtype=jnp.int32)[None, :] < group_counts[:, None]
        usable = jnp.repeat(usable, tile_len, axis=1)[:, None, :]
        scores = jnp.where(usable, scores, -jnp.inf)
        highest = jnp.max(scores, axis=-1, keepdims=True)
        raised = jnp.exp(scores - highest)
        weights = (raised / jnp.sum(raised, axis=-1, keepdims=True)).astype(jnp.bfloat16)
        mixed = jnp.einsum(
            "qtk,qkd->qtd", weights, gathered_values, preferred_element_type=jnp.float32
        )
        return mixed.astype(jnp.bfloat16)

    grouped = lax.map(one_group, jnp.arange(ntiles // QG, dtype=jnp.int32))
    return grouped.reshape(ntiles, tile_len, depth)


def attend_member(member, tile_rows, counts):
    ntiles = tile_rows.shape[0]
    local_rows = member.shape[1]
    tiles = member.reshape(3, ntiles, local_rows // ntiles, member.shape[2])
    full_out = attend_tiles(tiles[0], tiles[1], tiles[2], tile_rows, counts)
    return full_out.reshape(local_rows, member.shape[2])


def local(projected, gate, head_class, tile_lists, tile_counts):
    owners = lax.axis_size("seq")
    rank_here = lax.axis_index("seq")
    local_len = projected.shape[2]
    model_width = projected.shape[3]
    slot_count = -(-H // owners)
    spare = slot_count * owners - H
    heads_here = projected[0].reshape(3, local_len, H, HD)
    spread = jnp.pad(heads_here, ((0, 0), (0, 0), (0, spare), (0, 0)))
    spread = spread.reshape(3, local_len, slot_count, owners, HD).transpose(3, 2, 0, 1, 4)
    arrived = lax.all_to_all(spread, "seq", split_axis=0, concat_axis=3, tiled=True)
    results = []
    for slot_index in range(slot_count):
        head_id = slot_index * owners + rank_here
        member = arrived[0, slot_index]
        present = head_id < H
        source = jnp.minimum(head_id, H - 1)
        head_kind = lax.dynamic_index_in_dim(head_class, source, 0, keepdims=False)
        tile_rows = lax.dynamic_index_in_dim(tile_lists, head_kind, 0, keepdims=False)
        counts = lax.dynamic_index_in_dim(tile_counts, source, 0, keepdims=False)
        attended = attend_member(member, tile_rows, counts)
        gate_part = lax.dynamic_slice_in_dim(gate[0], source * HD, HD)
        attended = (gate_part.astype(jnp.float32)[None, :] * attended.astype(jnp.float32)).astype(
            jnp.bfloat16
        )
        results.append(jnp.where(present, attended, jnp.zeros_like(attended)))
    stacked = jnp.stack(results).reshape(slot_count, owners, local_len, HD)
    shifted = from_behind(stacked, "section", 1)
    returned = lax.all_to_all(shifted, "seq", split_axis=1, concat_axis=1, tiled=True)
    rows = returned.transpose(2, 0, 1, 3).reshape(local_len, slot_count * owners, HD)
    return rows[:, :H].reshape(local_len, model_width)[None]


def solution(mesh):
    placed = (P("section", None, "seq", None), P("section", None), P(), P(), P())
    return jax.shard_map(
        local, mesh=mesh, in_specs=placed, out_specs=P("section", "seq", None), check_vma=False
    )
```

profile of v0, /device:TPU:0, one launch (start us, length us, event | category | flops | bytes accessed | tf_op | source)
XLA Modules:
  0.0 455.8 jit_solution(10688093609297216342)
XLA Ops:
  0.0 12.7 %copy.24 = bf16[1,3,512,3072]{2,3,1,0:T(8,128)(2,1)} copy(bf16[1,3,512,3072]{3,2,1,0:T(8,128)(2,1)} %param.11) | data formatting | bytes 18874368 | tf_op args[0]
  12.7 12.6 %copy.25 = bf16[8,3,3,512,128]{4,3,2,1,0:T(8,128)(2,1)} copy(bf16[8,3,3,512,128]{3,4,0,1,2:T(8,128)(2,1)} %bitcast.141) | data formatting | bytes 18874368 | tf_op jit(solution)/shard_map/transpose | solution.py:69
  25.4 5.3 %all-to-all-start = ((bf16[8,3,3,512,128]{4,3,2,1,0:T(8,128)(2,1)}), bf16[8,3,3,512,128]{4,3,2,1,0:T(8,128)(2,1)}, u32[]{:S(2)}, u32[]{:S(2)}) async-start(bf16[8,3,3,512,128]{4,3,2,1,0:T(8,128)(2,1)} %copy.25), calls=%async_computation | async-start | bytes 18874368 | tf_op jit(solution)/shard_map/all_to_all | solution.py:70
  39.5 97.1 %all-to-all-done = bf16[8,3,3,512,128]{4,3,2,1,0:T(8,128)(2,1)} async-done(((bf16[8,3,3,512,128]{4,3,2,1,0:T(8,128)(2,1)}), bf16[8,3,3,512,128]{4,3,2,1,0:T(8,128)(2,1)}, u32[]{:S(2)}, u32[]{:S(2)}) %all-to-all-start) | async-done | bytes 9437216 | tf_op jit(solution)/shard_map/all_to_all | solution.py:70
  136.6 8.4 %copy.26 = bf16[8,3,3,512,128]{4,3,0,2,1:T(8,128)(2,1)} copy(bf16[8,3,3,512,128]{4,3,2,1,0:T(8,128)(2,1)} %all-to-all-done) | data formatting | bytes 18874368 | tf_op jit(solution)/shard_map/all_to_all | solution.py:70
  145.0 6.8 %fusion.60 = (bf16[1,1,1,4096,128]{4,3,2,1,0:T(8,128)(2,1)}, bf16[1,1,1,4096,128]{4,3,2,1,0:T(8,128)(2,1)S(1)}, bf16[1,1,1,4096,128]{4,3,2,1,0:T(8,128)(2,1)}, b...) fusion(bf16[1,3,3,4096,128]{4,3,2,1,0:T(8,128)(2,1)} %bitcast.140), kind=kLoop, calls=%fused_computation.100 | loop fusion | bytes 18874368 | tf_op jit(solution)/shard_map/slice | solution.py:56
  153.1 60.5 %while.31 = (s32[]{:T(128)}, bf16[4,8,128,128]{3,2,1,0:T(8,128)(2,1)}, s32[4]{0:T(128)S(1)}, s32[32]{0:T(128)S(1)}, bf16[32,128,128]{2,1,0:T(8,128)(2,1)}, /*ind...) while((s32[]{:T(128)}, ...), condition=%wide.region_7.8_spmd, body=%wide.region_4.7_spmd.sunk | while | flops 545392896 | bytes 34110136 | solution.py:48
  158.4 3.3 fusion.96
  163.8 4.3 fusion.97
  173.6 3.3 fusion.96
  179.0 4.3 fusion.97
  188.7 3.3 fusion.96
  194.1 4.4 fusion.97
  209.2 4.3 fusion.97
  214.7 60.4 %while.30 = (s32[]{:T(128)}, bf16[4,8,128,128]{3,2,1,0:T(8,128)(2,1)}, s32[4]{0:T(128)S(1)}, s32[32]{0:T(128)S(1)}, bf16[32,128,128]{2,1,0:T(8,128)(2,1)}, /*ind...) while((s32[]{:T(128)}, ...), condition=%wide.region_3.4_spmd, body=%wide.region_0.3_spmd.sunk | while | flops 545392896 | bytes 34110136 | solution.py:48
  225.5 4.3 fusion.91
  240.6 4.3 fusion.91
  255.7 4.3 fusion.91
  270.8 4.3 fusion.91
  276.4 53.6 %while.32 = (s32[]{:T(128)}, bf16[4,8,128,128]{3,2,1,0:T(8,128)(2,1)}, s32[4]{0:T(128)S(1)}, s32[32]{0:T(128)S(1)}, bf16[32,128,128]{2,1,0:T(8,128)(2,1)}, /*ind...) while((s32[]{:T(128)}, ...), condition=%wide.region_11.12_spmd, body=%wide.region_8.11_spmd.sunk | while | flops 545392896 | bytes 29915804 | solution.py:48
  281.9 3.3 fusion.102
  286.1 3.7 fusion.103
  295.3 3.3 fusion.102
  299.5 3.7 fusion.103
  308.7 3.3 fusion.102
  312.9 3.7 fusion.103
  322.1 3.3 fusion.102
  326.3 3.7 fusion.103
  336.3 67.2 %collective-permute-done = bf16[3,8,512,128]{3,2,1,0:T(8,128)(2,1)S(1)} collective-permute-done((bf16[3,8,512,128]{3,2,1,0:T(8,128)(2,1)S(1)}, bf16[3,8,512,128]{3,2,1,0:T(8,128)(2,1)S(1)}, u32[]{:S(2)}, u32[]{:S(2)}) %collective-permute-start) | collective-permute-done | bytes 3145760 | tf_op jit(solution)/shard_map/ppermute | solution.py:14
  403.8 42.7 %all_to_all.23 = bf16[3,8,512,128]{3,2,0,1:T(8,128)(2,1)} all-to-all(bf16[3,8,512,128]{3,2,0,1:T(8,128)(2,1)S(1)} %copy.30), channel_id=1, replica_groups=mesh['section'=4,'seq'=8] {'seq'}, dimensions={1} | all-to-all | bytes 6291456 | tf_op jit(solution)/shard_map/all_to_all | solution.py:88
  446.5 4.6 %copy.31 = bf16[3,8,512,128]{2,3,1,0:T(8,128)(2,1)} copy(bf16[3,8,512,128]{3,2,0,1:T(8,128)(2,1)} %all_to_all.23) | data formatting | bytes 6291456 | tf_op jit(solution)/shard_map/all_to_all | solution.py:88
  451.2 4.6 %copy.32 = bf16[1,512,3072]{2,1,0:T(8,128)(2,1)} copy(bf16[1,512,3072]{1,2,0:T(8,128)(2,1)} %bitcast.142) | data formatting | bytes 6291456 | tf_op jit(solution)/shard_map/broadcast_in_dim;reshape;reshape | solution.py:90
  (169 shorter events, 106.9 us)
Async XLA Ops:
  25.4 5.3 %copy-start.3 = (s32[24]{0:T(128)S(1)}, s32[24]{0:T(128)}, u32[]{:S(2)}) copy-start(s32[24]{0:T(128)} %param.13) | copy-start | bytes 292
  25.4 11.9 %copy-start.2 = (s32[2,32,8]{1,2,0:T(8,128)S(1)}, s32[2,32,8]{1,2,0:T(8,128)}, u32[]{:S(2)}) copy-start(s32[2,32,8]{1,2,0:T(8,128)} %param.14) | copy-start | bytes 6148
  25.4 111.2 %all-to-all-start = ((bf16[8,3,3,512,128]{4,3,2,1,0:T(8,128)(2,1)}), bf16[8,3,3,512,128]{4,3,2,1,0:T(8,128)(2,1)}, u32[]{:S(2)}, u32[]{:S(2)}) async-start(bf16[8,3,3,512,128]{4,3,2,1,0:T(8,128)(2,1)} %copy.25), calls=%async_computation | async-start | bytes 18874368 | tf_op jit(solution)/shard_map/all_to_all | solution.py:70
  158.4 3.3 copy-start.1
  173.6 3.3 copy-start.1
  188.7 3.3 copy-start.1
  203.8 3.3 copy-start.1
  220.1 3.3 copy-start
  235.2 3.3 copy-start
  250.3 3.3 copy-start
  265.4 3.3 copy-start
  276.4 53.6 %copy-start.4 = (f32[128]{0:T(128)S(1)}, f32[128]{0:T(128)}, u32[]{:S(2)}) copy-start(f32[128]{0:T(128)} %get-tuple-element.198) | copy-start | bytes 1540
  276.4 55.1 %copy-start.5 = (f32[128]{0:T(128)S(1)}, f32[128]{0:T(128)}, u32[]{:S(2)}) copy-start(f32[128]{0:T(128)} %get-tuple-element.197) | copy-start | bytes 1540
  276.4 55.1 %copy-start.6 = (f32[128]{0:T(128)S(1)}, f32[128]{0:T(128)}, u32[]{:S(2)}) copy-start(f32[128]{0:T(128)} %get-tuple-element.199) | copy-start | bytes 1540
  334.0 69.5 %collective-permute-start = (bf16[3,8,512,128]{3,2,1,0:T(8,128)(2,1)S(1)}, bf16[3,8,512,128]{3,2,1,0:T(8,128)(2,1)S(1)}, u32[]{:S(2)}, u32[]{:S(2)}) collective-permute-start(bf16[3,8,512,128]{3,2,1,0:T(8,128)(2,1)S(1)} %pad_maximum_fusion), channel_id=1, source_target_pairs={{24,0},{0,8},{8,16},{16,24},{25,1},{1,9},{9,17},{17,25},{26,2},{2,... | collective-permute-start | bytes 9437192 | tf_op jit(solution)/shard_map/ppermute | solution.py:14
where the time goes:
time: 458 us; the launch traced here: 456 us
  waiting for transfers between devices  164 us (36%)
  local copies, waits for them, and re-layouts  113 us (25%)
  matrix products  69.4 us (15%)
  other arithmetic  44.8 us (10%)
  blocking collectives  42.7 us (9%)
  loops' own time  8.39 us (2%)
  starting transfers between devices  7.64 us (2%)
  between operations  5.99 us (1%)
    all_to_all x1, waiting for transfers between devices, local(): lax.all_to_all(spread, 'seq', split_axis=0, concat_axis=3, tiled=True)  97.1 us
    ppermute x1, waiting for transfers between devices, from_behind(): return lax.ppermute(block, axis, route)  67.2 us
    dot_general x12, matrix products, one_group(): jnp.einsum('qtk,qkd->qtd', weights, gathered_values, preferred_element_ty...  49.5 us
    all_to_all x1, blocking collectives, local(): lax.all_to_all(shifted, 'seq', split_axis=1, concat_axis=1, tiled=True)  42.7 us
    sub x12, other arithmetic, one_group(): raised = jnp.exp(scores - highest)  39.2 us
    gather x12, local copies, waits for them, and re-layouts, one_group(): gathered_keys = key_tiles[group_rows].reshape(QG, kmax * tile_len, depth)  26.1 us
    gather x12, local copies, waits for them, and re-layouts, one_group(): value_tiles[group_rows].reshape(QG, kmax * tile_len, depth)  20.9 us
    dot_general x12, matrix products, one_group(): jnp.einsum('qtd,qkd->qtk', group_queries, gathered_keys, preferred_elemen...  19.9 us
  transfers between devices with their start and end apart: 2, of which 2 were waited for; matrix products, arithmetic and copies ran while one was open for 1% of the time, Pallas kernels for 0%

commit v1 on v0

v1 whole, which is shorter than its diff:
```python
import functools
import math

import jax
import jax.numpy as jnp
from jax import lax
from jax.experimental import pallas as pl
from jax.experimental.pallas import tpu as pltpu
from jax.sharding import PartitionSpec as P

HD = 128
MESH = pl.DeviceIdType.MESH


def relay_kernel(
    heads,
    owners,
    sections,
    slots,
    class_ref,
    lists_ref,
    counts_ref,
    gate_ref,
    fields_ref,
    out_ref,
    *scratch,
):
    members = scratch[:slots]
    staged = scratch[slots : 2 * slots]
    own_sem, in_send, in_recv, out_send, out_recv = scratch[2 * slots :]
    section = lax.axis_index("section")
    rank = lax.axis_index("seq")
    after = lax.rem(section + 1, sections)
    before = lax.rem(section + sections - 1, sections)
    chunk_tiles, tile_len = fields_ref.shape[1:3]
    local_len = chunk_tiles * tile_len
    kmax = lists_ref.shape[2]
    factor = HD ** (-0.5) * math.log2(math.e)
    valid = [min(owners, heads - slot * owners) for slot in range(slots)]

    def guarded(slot, member_rank, body):
        if valid[slot] == owners:
            body()
        else:
            pl.when(member_rank < valid[slot])(body)

    def columns(slot, member_rank):
        return pl.ds(pl.multiple_of((slot * owners + member_rank) * HD, HD), HD)

    def rows(member_rank):
        return pl.ds(pl.multiple_of(member_rank * local_len, local_len), local_len)

    def tiles(member_rank):
        return pl.ds(member_rank * chunk_tiles, chunk_tiles)

    def peer(distance):
        return lax.rem(rank + distance, owners)

    def in_copy(slot, target, source):
        return pltpu.make_async_remote_copy(
            src_ref=fields_ref.at[:, :, :, columns(slot, target)],
            dst_ref=members[slot].at[:, tiles(source)],
            send_sem=in_send.at[slot, target],
            recv_sem=in_recv.at[slot, source],
            device_id=(section, target),
            device_id_type=MESH,
        )

    def own_copy(slot):
        return pltpu.make_async_copy(
            fields_ref.at[:, :, :, columns(slot, rank)],
            members[slot].at[:, tiles(rank)],
            own_sem.at[slot],
        )

    def out_copy(slot, target, source):
        return pltpu.make_async_remote_copy(
            src_ref=staged[slot].at[rows(target), :],
            dst_ref=out_ref.at[:, columns(slot, source)],
            send_sem=out_send.at[slot, target],
            recv_sem=out_recv.at[slot, source],
            device_id=(after, target),
            device_id_type=MESH,
        )

    barrier = pltpu.get_barrier_semaphore()

    def greet_peer(distance, carry):
        pl.semaphore_signal(
            barrier, inc=1, device_id=(section, peer(distance)), device_id_type=MESH
        )
        return carry

    def greet_before(distance, carry):
        pl.semaphore_signal(
            barrier, inc=1, device_id=(before, peer(distance)), device_id_type=MESH
        )
        return carry

    lax.fori_loop(1, owners, greet_peer, 0)
    lax.fori_loop(0, owners, greet_before, 0)
    for slot in range(slots):
        guarded(slot, rank, lambda slot=slot: own_copy(slot).start())
    pl.semaphore_wait(barrier, 2 * owners - 1)

    def send_first(distance, carry):
        target = peer(distance)
        guarded(0, target, lambda: in_copy(0, target, rank).start())
        return carry

    lax.fori_loop(1, owners, send_first, 0)

    for slot in range(slots):
        if slot + 1 < slots:

            def send_next(distance, carry, slot=slot):
                target = peer(distance)
                guarded(slot, target, lambda: in_copy(slot, target, rank).wait_send())
                guarded(slot + 1, target, lambda: in_copy(slot + 1, target, rank).start())
                return carry

            lax.fori_loop(1, owners, send_next, 0)

        def attend_slot(slot=slot):
            own_copy(slot).wait()

            def receive(distance, carry):
                source = peer(distance)
                in_copy(slot, rank, source).wait_recv()
                return carry

            lax.fori_loop(1, owners, receive, 0)
            head = slot * owners + rank
            kind = class_ref[head]
            gate_part = gate_ref[:, pl.ds(pl.multiple_of(head * HD, HD), HD)].astype(jnp.float32)
            member = members[slot]

            def attend_tile(tile):
                here = pl.ds(pl.multiple_of(tile * tile_len, tile_len), tile_len)
                places = [
                    lists_ref[0, tile, j] + kind * (lists_ref[1, tile, j] - lists_ref[0, tile, j])
                    for j in range(kmax)
                ]
                queries = member[0, tile]
                keys = jnp.concatenate([member[1, place] for place in places], axis=0)
                values = jnp.concatenate([member[2, place] for place in places], axis=0)
                scores = lax.dot_general(
                    queries, keys, (((1,), (1,)), ((), ())), preferred_element_type=jnp.float32
                )
                index = lax.broadcasted_iota(jnp.int32, scores.shape, 1)
                scores = jnp.where(index < counts_ref[head, tile] * tile_len, scores, -jnp.inf)
                highest = jnp.max(scores, axis=-1, keepdims=True)
                raised = jnp.exp2((scores - highest) * factor)
                total = jnp.sum(raised, axis=-1, keepdims=True)
                weights = (raised * (1.0 / total)).astype(jnp.bfloat16)
                mixed = jnp.dot(weights, values, preferred_element_type=jnp.float32)
                mixed = mixed.astype(jnp.bfloat16).astype(jnp.float32)
                staged[slot][here, :] = (gate_part * mixed).astype(jnp.bfloat16)

            def attend_chunk(distance, carry):
                target = peer(distance)

                def step(i, inner):
                    attend_tile(target * chunk_tiles + 2 * i)
                    attend_tile(target * chunk_tiles + 2 * i + 1)
                    return inner

                if chunk_tiles % 2 == 0:
                    lax.fori_loop(0, chunk_tiles // 2, step, 0)
                else:
                    for i in range(chunk_tiles):
                        attend_tile(target * chunk_tiles + i)
                out_copy(slot, target, rank).start()
                return carry

            lax.fori_loop(0, owners, attend_chunk, 0)

        guarded(slot, rank, attend_slot)

    def finish_in(distance, carry):
        target = peer(distance)
        guarded(slots - 1, target, lambda: in_copy(slots - 1, target, rank).wait_send())
        return carry

    lax.fori_loop(1, owners, finish_in, 0)
    for slot in range(slots):

        def finish_send(slot=slot):
            def one(target, carry):
                out_copy(slot, target, rank).wait_send()
                return carry

            lax.fori_loop(0, owners, one, 0)

        guarded(slot, rank, finish_send)

        def finish_recv(source, carry, slot=slot):
            out_copy(slot, rank, source).wait_recv()
            return carry

        lax.fori_loop(0, valid[slot], finish_recv, 0)


def local(sections, owners, projected, gate, head_class, tile_lists, tile_counts):
    local_len, width = projected.shape[2:]
    heads = width // HD
    slots = -(-heads // owners)
    tokens = owners * local_len
    ntiles, kmax = tile_lists.shape[1:]
    tile_len = tokens // ntiles
    fields = projected.reshape(3, local_len // tile_len, tile_len, width)
    flops = 4 * slots * ntiles * tile_len * kmax * tile_len * HD
    smem = pl.BlockSpec(memory_space=pltpu.SMEM)
    out = pl.pallas_call(
        functools.partial(relay_kernel, heads, owners, sections, slots),
        out_shape=jax.ShapeDtypeStruct((local_len, width), jnp.bfloat16),
        in_specs=[smem, smem, smem, pl.BlockSpec(memory_space=pltpu.VMEM), pl.BlockSpec(memory_space=pl.ANY)],
        out_specs=pl.BlockSpec(memory_space=pl.ANY),
        scratch_shapes=[pltpu.VMEM((3, ntiles, tile_len, HD), jnp.bfloat16)] * slots
        + [pltpu.VMEM((tokens, HD), jnp.bfloat16)] * slots
        + [
            pltpu.SemaphoreType.DMA((slots,)),
            pltpu.SemaphoreType.DMA((slots, owners)),
            pltpu.SemaphoreType.DMA((slots, owners)),
            pltpu.SemaphoreType.DMA((slots, owners)),
            pltpu.SemaphoreType.DMA((slots, owners)),
        ],
        compiler_params=pltpu.CompilerParams(
            collective_id=0, has_side_effects=True, vmem_limit_bytes=56 * 1024 * 1024
        ),
        cost_estimate=pl.CostEstimate(
            flops=flops, bytes_accessed=8 * local_len * width, transcendentals=flops // (4 * HD)
        ),
    )(head_class, tile_lists, tile_counts, gate, fields)
    return out[None]


def solution(mesh):
    placed = (P("section", None, "seq", None), P("section", None), P(), P(), P())
    return jax.shard_map(
        functools.partial(local, mesh.shape["section"], mesh.shape["seq"]),
        mesh=mesh,
        in_specs=placed,
        out_specs=P("section", "seq", None),
        check_vma=False,
    )
```

time: 458 us -> 167 us (0.36)
  waiting for transfers between devices: 164 us -> 0 us
  Pallas kernels: 0 us -> 161 us
  local copies, waits for them, and re-layouts: 113 us -> 5.15 us
  matrix products: 69.4 us -> 0 us
  other arithmetic: 44.8 us -> 0 us
  blocking collectives: 42.7 us -> 0 us
  loops' own time: 8.39 us -> 0 us
  starting transfers between devices: 7.64 us -> 0 us
  between operations: 5.99 us -> 0.01 us
    pallas_call x0 -> x1, Pallas kernels: none -> 161 us  [local(): pl.pallas_call(functools.partial(relay_kernel, heads, owners, sections, s...]
    all_to_all x1 -> x0, waiting for transfers between devices: 97.1 us -> none  [local(): lax.all_to_all(spread, 'seq', split_axis=0, concat_axis=3, tiled=True)]
    dot_general x24 -> x0, matrix products: 69.4 us -> none  [the longest x12 49.5 us: one_group(): jnp.einsum('qtk,qkd->qtd', weights, gathered_values, preferred_element_ty...]
    ppermute x1 -> x0, waiting for transfers between devices: 67.2 us -> none  [from_behind(): return lax.ppermute(block, axis, route)]
    gather x24 -> x0, local copies, waits for them, and re-layouts: 47 us -> none  [the longest x12 26.1 us: one_group(): gathered_keys = key_tiles[group_rows].reshape(QG, kmax * tile_len, depth)]
    all_to_all x1 -> x0, blocking collectives: 42.7 us -> none  [local(): lax.all_to_all(shifted, 'seq', split_axis=1, concat_axis=1, tiled=True)]
    sub x12 -> x0, other arithmetic: 39.2 us -> none  [one_group(): raised = jnp.exp(scores - highest)]
    all_to_all x2 -> x0, local copies, waits for them, and re-layouts: 13.1 us -> none  [the longest x1 8.45 us: local(): lax.all_to_all(spread, 'seq', split_axis=0, concat_axis=3, tiled=True)]
  transfers between devices with their start and end apart: 2 -> 0, of which waited for: 2 -> 0; matrix products, arithmetic and copies ran while one was open for 1% -> 0% of each run, Pallas kernels for 0% -> 0%
where the time goes in v1:
time: 167 us; the launch traced here: 166 us
  Pallas kernels  161 us (96%)
  local copies, waits for them, and re-layouts  5.15 us (3%)
    pallas_call x1, Pallas kernels, local(): pl.pallas_call(functools.partial(relay_kernel, heads, owners, sections, s...  161 us
    unnamed x2, local copies, waits for them, and re-layouts  5.15 us

profile of v1, /device:TPU:0, one launch (start us, length us, event | category | flops | bytes accessed | tf_op | source)
XLA Modules:
  0.0 166.4 jit_solution(11697651095858599598)
XLA Ops:
  0.0 1.4 copy.6.lists_ref
  1.4 161.2 %shard_map.55 = bf16[512,3072]{1,0:T(8,128)(2,1)} custom-call(s32[24]{0:T(128)} %class_ref.1, s32[2,32,8]{2,1,0:T(8,128)} %copy.6.lists_ref, s32[24,32]{1,0:T(8,128)} %counts_ref.1, bf16[1,3072]{1,0:T(2,128)(2,1)} %gate_ref.1, bf16[3,4,128,3072]{3,2,1,0:T(8,128)(2,1)} %bitcast.3), custom_call_target="tpu_custom_call" | custom-call | flops 6442450944 | bytes 12582912 | tf_op jit(solution)/shard_map/pallas_call | solution.py:214
  162.6 3.8 %copy.8 = bf16[1,512,3072]{2,1,0:T(8,128)(2,1)} copy(bf16[1,512,3072]{2,1,0:T(8,128)(2,1)} %bitcast.2) | data formatting | bytes 6291456

commit v2 on v1

v2 whole, which is shorter than its diff:
```python
import functools
import math

import jax
import jax.numpy as jnp
from jax import lax
from jax.experimental import pallas as pl
from jax.experimental.pallas import tpu as pltpu
from jax.sharding import PartitionSpec as P

HD = 128
MESH = pl.DeviceIdType.MESH


def relay_kernel(
    heads,
    owners,
    sections,
    slots,
    class_ref,
    lists_ref,
    counts_ref,
    gate_ref,
    fields_ref,
    out_ref,
    *scratch,
):
    queries = scratch[:slots]
    pairs = scratch[slots : 2 * slots]
    staged = scratch[2 * slots : 3 * slots]
    own_sem, q_send, q_recv, kv_send, kv_recv, out_send, out_recv = scratch[3 * slots :]
    section = lax.axis_index("section")
    rank = lax.axis_index("seq")
    after = lax.rem(section + 1, sections)
    before = lax.rem(section + sections - 1, sections)
    chunk_tiles, tile_len = fields_ref.shape[1:3]
    local_len = chunk_tiles * tile_len
    kmax = lists_ref.shape[1]
    factor = HD ** (-0.5) * math.log2(math.e)
    valid = [min(owners, heads - slot * owners) for slot in range(slots)]
    half = owners // 2

    def guarded(slot, member_rank, body):
        if valid[slot] == owners:
            body()
        else:
            pl.when(member_rank < valid[slot])(body)

    def columns(slot, member_rank):
        return pl.ds(pl.multiple_of((slot * owners + member_rank) * HD, HD), HD)

    def rows(member_rank):
        return pl.ds(pl.multiple_of(member_rank * local_len, local_len), local_len)

    def tiles(member_rank):
        return pl.ds(member_rank * chunk_tiles, chunk_tiles)

    def peer(step):
        distance = 2 * lax.rem(step, half) + lax.div(step, half)
        other = 0
        bit = 1
        while bit < owners:
            other = other + bit * lax.rem(lax.div(rank, bit) + lax.div(distance, bit), 2)
            bit *= 2
        return other

    def q_copy(slot, target, source):
        return pltpu.make_async_remote_copy(
            src_ref=fields_ref.at[0, :, :, columns(slot, target)],
            dst_ref=queries[slot].at[tiles(source)],
            send_sem=q_send.at[slot, target],
            recv_sem=q_recv.at[slot, source],
            device_id=(section, target),
            device_id_type=MESH,
        )

    def kv_copy(slot, target, source):
        return pltpu.make_async_remote_copy(
            src_ref=fields_ref.at[pl.ds(1, 2), :, :, columns(slot, target)],
            dst_ref=pairs[slot].at[:, tiles(source)],
            send_sem=kv_send.at[slot, target],
            recv_sem=kv_recv.at[slot, source],
            device_id=(section, target),
            device_id_type=MESH,
        )

    def own_q_copy(slot):
        return pltpu.make_async_copy(
            fields_ref.at[0, :, :, columns(slot, rank)],
            queries[slot].at[tiles(rank)],
            own_sem.at[slot, 0],
        )

    def own_kv_copy(slot):
        return pltpu.make_async_copy(
            fields_ref.at[pl.ds(1, 2), :, :, columns(slot, rank)],
            pairs[slot].at[:, tiles(rank)],
            own_sem.at[slot, 1],
        )

    def out_copy(slot, target, source):
        return pltpu.make_async_remote_copy(
            src_ref=staged[slot].at[rows(target), :],
            dst_ref=out_ref.at[:, columns(slot, source)],
            send_sem=out_send.at[slot, target],
            recv_sem=out_recv.at[slot, source],
            device_id=(after, target),
            device_id_type=MESH,
        )

    def each(first, last, body):
        def step(i, carry):
            body(peer(i))
            return carry

        lax.fori_loop(first, last, step, 0)

    def to_peers(slot, first, last, body):
        each(first, last, lambda target: guarded(slot, target, lambda: body(target)))

    barrier = pltpu.get_barrier_semaphore()

    def greet(place):
        def one(target):
            pl.semaphore_signal(barrier, inc=1, device_id=(place, target), device_id_type=MESH)

        return one

    each(1, owners, greet(section))
    each(0, owners, greet(before))

    def start_own(slot):
        own_q_copy(slot).start()
        own_kv_copy(slot).start()

    for slot in range(slots):
        guarded(slot, rank, functools.partial(start_own, slot))
    pl.semaphore_wait(barrier, 2 * owners - 1)

    to_peers(0, 1, owners, lambda target: kv_copy(0, target, rank).start())
    if slots > 1:
        to_peers(0, 1, owners, lambda target: q_copy(0, target, rank).start())

    for slot in range(slots):
        final = slot == slots - 1

        def kv_sent(target, slot=slot):
            kv_copy(slot, target, rank).wait_send()

        def q_start(target, slot=slot):
            q_copy(slot, target, rank).start()

        def q_sent(target, slot=slot):
            q_copy(slot, target, rank).wait_send()

        def gather_pairs(slot=slot):
            own_q_copy(slot).wait()
            own_kv_copy(slot).wait()
            each(1, owners, lambda source: kv_copy(slot, rank, source).wait_recv())

        def attend_chunks(first, last, slot=slot):
            head = slot * owners + rank
            kind = class_ref[head]
            gate_part = gate_ref[:, pl.ds(pl.multiple_of(head * HD, HD), HD)].astype(jnp.float32)

            def attend_tile(tile):
                here = pl.ds(pl.multiple_of(tile * tile_len, tile_len), tile_len)
                places = [
                    lists_ref[0, j, tile] + kind * (lists_ref[1, j, tile] - lists_ref[0, j, tile])
                    for j in range(kmax)
                ]
                keys = jnp.concatenate([pairs[slot][0, place] for place in places], axis=0)
                values = jnp.concatenate([pairs[slot][1, place] for place in places], axis=0)
                scores = lax.dot_general(
                    queries[slot][tile],
                    keys,
                    (((1,), (1,)), ((), ())),
                    preferred_element_type=jnp.float32,
                )
                index = lax.broadcasted_iota(jnp.int32, scores.shape, 1)
                scores = jnp.where(index < counts_ref[head, tile] * tile_len, scores, -jnp.inf)
                highest = jnp.max(scores, axis=-1, keepdims=True)
                raised = jnp.exp2((scores - highest) * factor)
                total = jnp.sum(raised, axis=-1, keepdims=True)
                weights = (raised * (1.0 / total)).astype(jnp.bfloat16)
                mixed = jnp.dot(weights, values, preferred_element_type=jnp.float32)
                mixed = mixed.astype(jnp.bfloat16).astype(jnp.float32)
                staged[slot][here, :] = (gate_part * mixed).astype(jnp.bfloat16)

            def attend_chunk(step, carry):
                target = peer(step)

                @pl.when(step > 0)
                def _():
                    q_copy(slot, rank, target).wait_recv()

                def attend_two(i, inner):
                    attend_tile(target * chunk_tiles + 2 * i)
                    attend_tile(target * chunk_tiles + 2 * i + 1)
                    return inner

                if chunk_tiles % 2 == 0:
                    lax.fori_loop(0, chunk_tiles // 2, attend_two, 0)
                else:
                    for i in range(chunk_tiles):
                        attend_tile(target * chunk_tiles + i)
                out_copy(slot, target, rank).start()
                return carry

            lax.fori_loop(first, last, attend_chunk, 0)

        if not final:

            def kv_next(target, slot=slot):
                guarded(slot, target, lambda: kv_copy(slot, target, rank).wait_send())
                guarded(slot + 1, target, lambda: kv_copy(slot + 1, target, rank).start())

            each(1, owners, kv_next)
            guarded(slot, rank, gather_pairs)
            guarded(slot, rank, functools.partial(attend_chunks, 0, owners))
            to_peers(slot, 1, owners, q_sent)
            if slot + 1 < slots - 1:
                to_peers(
                    slot + 1, 1, owners, lambda target: q_copy(slot + 1, target, rank).start()
                )
        else:

            def q_after_kv(target):
                kv_sent(target)
                q_start(target)

            to_peers(slot, 1, half, q_after_kv)
            guarded(slot, rank, gather_pairs)
            guarded(slot, rank, functools.partial(attend_chunks, 0, 1))
            to_peers(slot, 1, half, q_sent)
            to_peers(slot, half, owners, q_after_kv)
            guarded(slot, rank, functools.partial(attend_chunks, 1, owners))
            to_peers(slot, half, owners, q_sent)

    for slot in range(slots):

        def finish_send(slot=slot):
            each(0, owners, lambda target: out_copy(slot, target, rank).wait_send())

        guarded(slot, rank, finish_send)

        def finish_recv(source, carry, slot=slot):
            out_copy(slot, rank, source).wait_recv()
            return carry

        lax.fori_loop(0, valid[slot], finish_recv, 0)


def local(sections, owners, projected, gate, head_class, tile_lists, tile_counts):
    local_len, width = projected.shape[2:]
    heads = width // HD
    slots = -(-heads // owners)
    tokens = owners * local_len
    ntiles, kmax = tile_lists.shape[1:]
    tile_len = tokens // ntiles
    fields = projected.reshape(3, local_len // tile_len, tile_len, width)
    flops = 4 * slots * ntiles * tile_len * kmax * tile_len * HD
    smem = pl.BlockSpec(memory_space=pltpu.SMEM)
    out = pl.pallas_call(
        functools.partial(relay_kernel, heads, owners, sections, slots),
        out_shape=jax.ShapeDtypeStruct((local_len, width), jnp.bfloat16),
        in_specs=[smem, smem, smem, pl.BlockSpec(memory_space=pltpu.VMEM), pl.BlockSpec(memory_space=pl.ANY)],
        out_specs=pl.BlockSpec(memory_space=pl.ANY),
        scratch_shapes=[pltpu.VMEM((ntiles, tile_len, HD), jnp.bfloat16)] * slots
        + [pltpu.VMEM((2, ntiles, tile_len, HD), jnp.bfloat16)] * slots
        + [pltpu.VMEM((tokens, HD), jnp.bfloat16)] * slots
        + [
            pltpu.SemaphoreType.DMA((slots, 2)),
            pltpu.SemaphoreType.DMA((slots, owners)),
            pltpu.SemaphoreType.DMA((slots, owners)),
            pltpu.SemaphoreType.DMA((slots, owners)),
            pltpu.SemaphoreType.DMA((slots, owners)),
            pltpu.SemaphoreType.DMA((slots, owners)),
            pltpu.SemaphoreType.DMA((slots, owners)),
        ],
        compiler_params=pltpu.CompilerParams(
            collective_id=0, has_side_effects=True, vmem_limit_bytes=56 * 1024 * 1024
        ),
        cost_estimate=pl.CostEstimate(
            flops=flops, bytes_accessed=8 * local_len * width, transcendentals=flops // (4 * HD)
        ),
    )(head_class, tile_lists.transpose(0, 2, 1), tile_counts, gate, fields)
    return out[None]


def solution(mesh):
    placed = (P("section", None, "seq", None), P("section", None), P(), P(), P())
    return jax.shard_map(
        functools.partial(local, mesh.shape["section"], mesh.shape["seq"]),
        mesh=mesh,
        in_specs=placed,
        out_specs=P("section", "seq", None),
        check_vma=False,
    )
```

time: 167 us -> 161 us (0.964)
  Pallas kernels: 161 us -> 157 us
    pallas_call x1, Pallas kernels: 161 us -> 157 us  [local(): pl.pallas_call(functools.partial(relay_kernel, heads, owners, sections, s...]
    unnamed x2 -> x1, local copies, waits for them, and re-layouts: 5.15 us -> 3.76 us
where the time goes in v2:
time: 161 us
  Pallas kernels  157 us (98%)
  local copies, waits for them, and re-layouts  3.76 us (2%)
    pallas_call x1, Pallas kernels, local(): pl.pallas_call(functools.partial(relay_kernel, heads, owners, sections, s...  157 us
    unnamed x1, local copies, waits for them, and re-layouts  3.76 us

profile of v2, /device:TPU:0, one launch (start us, length us, event | category | flops | bytes accessed | tf_op | source)
XLA Modules:
  0.0 161.0 jit_solution(11833009818228269410)
XLA Ops:
  0.0 157.2 %shard_map.55 = bf16[512,3072]{1,0:T(8,128)(2,1)} custom-call(s32[24]{0:T(128)} %class_ref.1, s32[2,8,32]{2,1,0:T(8,128)} %bitcast.5, s32[24,32]{1,0:T(8,128)} %counts_ref.1, bf16[1,3072]{1,0:T(2,128)(2,1)} %gate_ref.1, bf16[3,4,128,3072]{3,2,1,0:T(8,128)(2,1)} %bitcast.4), custom_call_target="tpu_custom_call" | custom-call | flops 6442450944 | bytes 12582912 | tf_op jit(solution)/shard_map/pallas_call | solution.py:264
  157.2 3.8 %copy.7 = bf16[1,512,3072]{2,1,0:T(8,128)(2,1)} copy(bf16[1,512,3072]{2,1,0:T(8,128)(2,1)} %bitcast.3) | data formatting | bytes 6291456

commit v3 on v2

--- a/solution.py
+++ b/solution.py
@@ -28,17 +28,19 @@
     queries = scratch[:slots]
     pairs = scratch[slots : 2 * slots]
     staged = scratch[2 * slots : 3 * slots]
-    own_sem, q_send, q_recv, kv_send, kv_recv, out_send, out_recv = scratch[3 * slots :]
+    usable = scratch[3 * slots]
+    own_sem, q_send, q_recv, kv_send, kv_recv, out_send, out_recv = scratch[3 * slots + 1 :]
     section = lax.axis_index("section")
     rank = lax.axis_index("seq")
     after = lax.rem(section + 1, sections)
     before = lax.rem(section + sections - 1, sections)
     chunk_tiles, tile_len = fields_ref.shape[1:3]
     local_len = chunk_tiles * tile_len
-    kmax = lists_ref.shape[1]
+    kmax, ntiles = lists_ref.shape[1:]
     factor = HD ** (-0.5) * math.log2(math.e)
     valid = [min(owners, heads - slot * owners) for slot in range(slots)]
     half = owners // 2
+    chip, core = lax.div(rank, 2), lax.rem(rank, 2)
 
     def guarded(slot, member_rank, body):
         if valid[slot] == owners:
@@ -55,14 +57,16 @@
     def tiles(member_rank):
         return pl.ds(member_rank * chunk_tiles, chunk_tiles)
 
-    def peer(step):
-        distance = 2 * lax.rem(step, half) + lax.div(step, half)
+    def flipped(index, distance):
         other = 0
         bit = 1
-        while bit < owners:
-            other = other + bit * lax.rem(lax.div(rank, bit) + lax.div(distance, bit), 2)
+        while bit < half:
+            other = other + bit * lax.rem(lax.div(index, bit) + lax.div(distance, bit), 2)
             bit *= 2
         return other
+
+    def peer(step):
+        return 2 * flipped(chip, lax.rem(step, half)) + lax.rem(core + lax.div(step, half), 2)
 
     def q_copy(slot, target, source):
         return pltpu.make_async_remote_copy(
@@ -115,8 +119,43 @@
 
         lax.fori_loop(first, last, step, 0)
 
-    def to_peers(slot, first, last, body):
-        each(first, last, lambda target: guarded(slot, target, lambda: body(target)))
+    def to_core(slot, side, body):
+        def one(target):
+            guarded(slot, target, lambda: body(target))
+
+        pl.when(core != side)(lambda: one(2 * chip + side))
+
+        def step(distance, carry):
+            one(2 * flipped(chip, distance) + side)
+            return carry
+
+        lax.fori_loop(1, half, step, 0)
+
+    def sent_then(copy, slot, side, following):
+        def sent(distance):
+            target = 2 * flipped(chip, distance) + side
+            guarded(slot, target, lambda: copy(slot, target, rank).wait_send())
+
+        def start(distance):
+            target = 2 * flipped(chip, distance) + 1 - side
+            guarded(following, target, lambda: copy(following, target, rank).start())
+
+        pl.when(core != side)(lambda: sent(0))
+        if following < slots:
+            pl.when(core == side)(lambda: start(0))
+
+        def step(distance, carry):
+            sent(distance)
+            if following < slots:
+                start(distance)
+            return carry
+
+        lax.fori_loop(1, half, step, 0)
+
+    usable[0] = jnp.zeros((tile_len, HD), jnp.bfloat16)
+    usable[1] = jnp.ones((tile_len, HD), jnp.bfloat16)
+    for slot in range(slots):
+        pairs[slot][:, ntiles] = jnp.zeros((2, tile_len, HD), jnp.bfloat16)
 
     barrier = pltpu.get_barrier_semaphore()
 
@@ -137,22 +176,10 @@
         guarded(slot, rank, functools.partial(start_own, slot))
     pl.semaphore_wait(barrier, 2 * owners - 1)
 
-    to_peers(0, 1, owners, lambda target: kv_copy(0, target, rank).start())
-    if slots > 1:
-        to_peers(0, 1, owners, lambda target: q_copy(0, target, rank).start())
+    to_core(0, 0, lambda target: kv_copy(0, target, rank).start())
+    to_core(0, 0, lambda target: q_copy(0, target, rank).start())
 
     for slot in range(slots):
-        final = slot == slots - 1
-
-        def kv_sent(target, slot=slot):
-            kv_copy(slot, target, rank).wait_send()
-
-        def q_start(target, slot=slot):
-            q_copy(slot, target, rank).start()
-
-        def q_sent(target, slot=slot):
-            q_copy(slot, target, rank).wait_send()
-
         def gather_pairs(slot=slot):
             own_q_copy(slot).wait()
             own_kv_copy(slot).wait()
@@ -165,25 +192,29 @@
 
             def attend_tile(tile):
                 here = pl.ds(pl.multiple_of(tile * tile_len, tile_len), tile_len)
-                places = [
-                    lists_ref[0, j, tile] + kind * (lists_ref[1, j, tile] - lists_ref[0, j, tile])
-                    for j in range(kmax)
-                ]
+                count = counts_ref[head, tile]
+                places, fillers, flags = [tile], [tile], [1]
+                for j in range(1, kmax):
+                    listed = lists_ref[0, j, tile] + kind * (
+                        lists_ref[1, j, tile] - lists_ref[0, j, tile]
+                    )
+                    places.append(jnp.where(j < count, listed, tile))
+                    fillers.append(jnp.where(j < count, listed, ntiles))
+                    flags.append(jnp.where(j < count, 1, 0))
                 keys = jnp.concatenate([pairs[slot][0, place] for place in places], axis=0)
-                values = jnp.concatenate([pairs[slot][1, place] for place in places], axis=0)
+                values = jnp.concatenate([pairs[slot][1, place] for place in fillers], axis=0)
+                marks = jnp.concatenate([usable[flag] for flag in flags], axis=0)
+                values = jnp.concatenate([values, marks], axis=1)
                 scores = lax.dot_general(
                     queries[slot][tile],
                     keys,
                     (((1,), (1,)), ((), ())),
                     preferred_element_type=jnp.float32,
                 )
-                index = lax.broadcasted_iota(jnp.int32, scores.shape, 1)
-                scores = jnp.where(index < counts_ref[head, tile] * tile_len, scores, -jnp.inf)
                 highest = jnp.max(scores, axis=-1, keepdims=True)
-                raised = jnp.exp2((scores - highest) * factor)
-                total = jnp.sum(raised, axis=-1, keepdims=True)
-                weights = (raised * (1.0 / total)).astype(jnp.bfloat16)
-                mixed = jnp.dot(weights, values, preferred_element_type=jnp.float32)
+                raised = jnp.exp2((scores - highest) * factor).astype(jnp.bfloat16)
+                mixed = jnp.dot(raised, values, preferred_element_type=jnp.float32)
+                mixed = mixed[:, :HD] / mixed[:, HD:]
                 mixed = mixed.astype(jnp.bfloat16).astype(jnp.float32)
                 staged[slot][here, :] = (gate_part * mixed).astype(jnp.bfloat16)
 
@@ -209,33 +240,18 @@
 
             lax.fori_loop(first, last, attend_chunk, 0)
 
-        if not final:
-
-            def kv_next(target, slot=slot):
-                guarded(slot, target, lambda: kv_copy(slot, target, rank).wait_send())
-                guarded(slot + 1, target, lambda: kv_copy(slot + 1, target, rank).start())
-
-            each(1, owners, kv_next)
-            guarded(slot, rank, gather_pairs)
-            guarded(slot, rank, functools.partial(attend_chunks, 0, owners))
-            to_peers(slot, 1, owners, q_sent)
-            if slot + 1 < slots - 1:
-                to_peers(
-                    slot + 1, 1, owners, lambda target: q_copy(slot + 1, target, rank).start()
-                )
-        else:
-
-            def q_after_kv(target):
-                kv_sent(target)
-                q_start(target)
-
-            to_peers(slot, 1, half, q_after_kv)
-            guarded(slot, rank, gather_pairs)
-            guarded(slot, rank, functools.partial(attend_chunks, 0, 1))
-            to_peers(slot, 1, half, q_sent)
-            to_peers(slot, half, owners, q_after_kv)
-            guarded(slot, rank, functools.partial(attend_chunks, 1, owners))
-            to_peers(slot, half, owners, q_sent)
+        def attend_slot(slot=slot, attend_chunks=attend_chunks, gather_pairs=gather_pairs):
+            gather_pairs()
+            attend_chunks(0, owners)
+
+        for side in range(2):
+            following = slot + side
+            for copy in (kv_copy, q_copy):
+                sent_then(copy, slot, side, following)
+
+            @pl.when(core == side)
+            def _(slot=slot, attend_slot=attend_slot):
+                guarded(slot, rank, attend_slot)
 
     for slot in range(slots):
 
@@ -267,8 +283,9 @@
         in_specs=[smem, smem, smem, pl.BlockSpec(memory_space=pltpu.VMEM), pl.BlockSpec(memory_space=pl.ANY)],
         out_specs=pl.BlockSpec(memory_space=pl.ANY),
         scratch_shapes=[pltpu.VMEM((ntiles, tile_len, HD), jnp.bfloat16)] * slots
-        + [pltpu.VMEM((2, ntiles, tile_len, HD), jnp.bfloat16)] * slots
+        + [pltpu.VMEM((2, ntiles + 1, tile_len, HD), jnp.bfloat16)] * slots
         + [pltpu.VMEM((tokens, HD), jnp.bfloat16)] * slots
+        + [pltpu.VMEM((2, tile_len, HD), jnp.bfloat16)]
         + [
             pltpu.SemaphoreType.DMA((slots, 2)),
             pltpu.SemaphoreType.DMA((slots, owners)),

time: 161 us -> 165 us (1.025)
  Pallas kernels: 157 us -> 161 us
    pallas_call x1, Pallas kernels: 157 us -> 161 us  [local(): pl.pallas_call(functools.partial(relay_kernel, heads, owners, sections, s...]
where the time goes in v3:
time: 165 us
  Pallas kernels  161 us (98%)
  local copies, waits for them, and re-layouts  3.76 us (2%)
    pallas_call x1, Pallas kernels, local(): pl.pallas_call(functools.partial(relay_kernel, heads, owners, sections, s...  161 us
    unnamed x1, local copies, waits for them, and re-layouts  3.76 us

profile of v3, /device:TPU:0, one launch (start us, length us, event | category | flops | bytes accessed | tf_op | source)
XLA Modules:
  0.0 164.8 jit_solution(2145703575090252755)
XLA Ops:
  0.0 161.1 %shard_map.55 = bf16[512,3072]{1,0:T(8,128)(2,1)} custom-call(s32[24]{0:T(128)} %class_ref.1, s32[2,8,32]{2,1,0:T(8,128)} %bitcast.5, s32[24,32]{1,0:T(8,128)} %counts_ref.1, bf16[1,3072]{1,0:T(2,128)(2,1)} %gate_ref.1, bf16[3,4,128,3072]{3,2,1,0:T(8,128)(2,1)} %bitcast.4), custom_call_target="tpu_custom_call" | custom-call | flops 6442450944 | bytes 12582912 | tf_op jit(solution)/shard_map/pallas_call | solution.py:280
  161.1 3.8 %copy.7 = bf16[1,512,3072]{2,1,0:T(8,128)(2,1)} copy(bf16[1,512,3072]{2,1,0:T(8,128)(2,1)} %bitcast.3) | data formatting | bytes 6291456

commit v4 on v3

--- a/solution.py
+++ b/solution.py
@@ -131,23 +131,16 @@
 
         lax.fori_loop(1, half, step, 0)
 
-    def sent_then(copy, slot, side, following):
-        def sent(distance):
-            target = 2 * flipped(chip, distance) + side
+    def sent_then(copy, slot, side):
+        def one(target):
             guarded(slot, target, lambda: copy(slot, target, rank).wait_send())
-
-        def start(distance):
-            target = 2 * flipped(chip, distance) + 1 - side
-            guarded(following, target, lambda: copy(following, target, rank).start())
-
-        pl.when(core != side)(lambda: sent(0))
-        if following < slots:
-            pl.when(core == side)(lambda: start(0))
+            if slot + 1 < slots:
+                guarded(slot + 1, target, lambda: copy(slot + 1, target, rank).start())
+
+        pl.when(core != side)(lambda: one(2 * chip + side))
 
         def step(distance, carry):
-            sent(distance)
-            if following < slots:
-                start(distance)
+            one(2 * flipped(chip, distance) + side)
             return carry
 
         lax.fori_loop(1, half, step, 0)
@@ -176,8 +169,9 @@
         guarded(slot, rank, functools.partial(start_own, slot))
     pl.semaphore_wait(barrier, 2 * owners - 1)
 
-    to_core(0, 0, lambda target: kv_copy(0, target, rank).start())
-    to_core(0, 0, lambda target: q_copy(0, target, rank).start())
+    for side in range(2):
+        to_core(0, side, lambda target: kv_copy(0, target, rank).start())
+        to_core(0, side, lambda target: q_copy(0, target, rank).start())
 
     for slot in range(slots):
         def gather_pairs(slot=slot):
@@ -245,9 +239,8 @@
             attend_chunks(0, owners)
 
         for side in range(2):
-            following = slot + side
             for copy in (kv_copy, q_copy):
-                sent_then(copy, slot, side, following)
+                sent_then(copy, slot, side)
 
             @pl.when(core == side)
             def _(slot=slot, attend_slot=attend_slot):

time: 165 us -> 165 us (level)
  no operation moved by 1% of the time
where the time goes in v4:
time: 165 us
  Pallas kernels  161 us (98%)
  local copies, waits for them, and re-layouts  3.76 us (2%)
    pallas_call x1, Pallas kernels, local(): pl.pallas_call(functools.partial(relay_kernel, heads, owners, sections, s...  161 us
    unnamed x1, local copies, waits for them, and re-layouts  3.76 us

profile of v4, /device:TPU:0, one launch (start us, length us, event | category | flops | bytes accessed | tf_op | source)
XLA Modules:
  0.0 165.0 jit_solution(645224435152161435)
XLA Ops:
  0.0 161.2 %shard_map.55 = bf16[512,3072]{1,0:T(8,128)(2,1)} custom-call(s32[24]{0:T(128)} %class_ref.1, s32[2,8,32]{2,1,0:T(8,128)} %bitcast.5, s32[24,32]{1,0:T(8,128)} %counts_ref.1, bf16[1,3072]{1,0:T(2,128)(2,1)} %gate_ref.1, bf16[3,4,128,3072]{3,2,1,0:T(8,128)(2,1)} %bitcast.4), custom_call_target="tpu_custom_call" | custom-call | flops 6442450944 | bytes 12582912 | tf_op jit(solution)/shard_map/pallas_call | solution.py:273
  161.2 3.8 %copy.7 = bf16[1,512,3072]{2,1,0:T(8,128)(2,1)} copy(bf16[1,512,3072]{2,1,0:T(8,128)(2,1)} %bitcast.3) | data formatting | bytes 6291456

commit v5 on v2

--- a/solution.py
+++ b/solution.py
@@ -28,7 +28,8 @@
     queries = scratch[:slots]
     pairs = scratch[slots : 2 * slots]
     staged = scratch[2 * slots : 3 * slots]
-    own_sem, q_send, q_recv, kv_send, kv_recv, out_send, out_recv = scratch[3 * slots :]
+    parcels, landed, own_sem, pack_sem, land_sem = scratch[3 * slots : 3 * slots + 5]
+    q_send, q_recv, kv_send, kv_recv, out_send, out_recv = scratch[3 * slots + 5 :]
     section = lax.axis_index("section")
     rank = lax.axis_index("seq")
     after = lax.rem(section + 1, sections)
@@ -66,7 +67,7 @@
 
     def q_copy(slot, target, source):
         return pltpu.make_async_remote_copy(
-            src_ref=fields_ref.at[0, :, :, columns(slot, target)],
+            src_ref=parcels.at[slot * owners + target, 0],
             dst_ref=queries[slot].at[tiles(source)],
             send_sem=q_send.at[slot, target],
             recv_sem=q_recv.at[slot, source],
@@ -76,7 +77,7 @@
 
     def kv_copy(slot, target, source):
         return pltpu.make_async_remote_copy(
-            src_ref=fields_ref.at[pl.ds(1, 2), :, :, columns(slot, target)],
+            src_ref=parcels.at[slot * owners + target, pl.ds(1, 2)],
             dst_ref=pairs[slot].at[:, tiles(source)],
             send_sem=kv_send.at[slot, target],
             recv_sem=kv_recv.at[slot, source],
@@ -84,6 +85,20 @@
             device_id_type=MESH,
         )
 
+    def pack_copy(slot, target):
+        return pltpu.make_async_copy(
+            fields_ref.at[:, :, :, columns(slot, target)],
+            parcels.at[slot * owners + target],
+            pack_sem.at[slot, target],
+        )
+
+    def land_copy(slot, source):
+        return pltpu.make_async_copy(
+            landed.at[slot * owners + source],
+            out_ref.at[:, columns(slot, source)],
+            land_sem.at[slot, source],
+        )
+
     def own_q_copy(slot):
         return pltpu.make_async_copy(
             fields_ref.at[0, :, :, columns(slot, rank)],
@@ -101,7 +116,7 @@
     def out_copy(slot, target, source):
         return pltpu.make_async_remote_copy(
             src_ref=staged[slot].at[rows(target), :],
-            dst_ref=out_ref.at[:, columns(slot, source)],
+            dst_ref=landed.at[slot * owners + source],
             send_sem=out_send.at[slot, target],
             recv_sem=out_recv.at[slot, source],
             device_id=(after, target),
@@ -134,10 +149,15 @@
         own_kv_copy(slot).start()
 
     for slot in range(slots):
+        to_peers(slot, 1, owners, lambda target: pack_copy(slot, target).start())
         guarded(slot, rank, functools.partial(start_own, slot))
     pl.semaphore_wait(barrier, 2 * owners - 1)
 
-    to_peers(0, 1, owners, lambda target: kv_copy(0, target, rank).start())
+    def kv_start(slot, target):
+        pack_copy(slot, target).wait()
+        kv_copy(slot, target, rank).start()
+
+    to_peers(0, 1, owners, functools.partial(kv_start, 0))
     if slots > 1:
         to_peers(0, 1, owners, lambda target: q_copy(0, target, rank).start())
 
@@ -213,7 +233,7 @@
 
             def kv_next(target, slot=slot):
                 guarded(slot, target, lambda: kv_copy(slot, target, rank).wait_send())
-                guarded(slot + 1, target, lambda: kv_copy(slot + 1, target, rank).start())
+                guarded(slot + 1, target, lambda: kv_start(slot + 1, target))
 
             each(1, owners, kv_next)
             guarded(slot, rank, gather_pairs)
@@ -239,16 +259,24 @@
 
     for slot in range(slots):
 
+        def finish_recv(source, carry, slot=slot):
+            out_copy(slot, rank, source).wait_recv()
+            land_copy(slot, source).start()
+            return carry
+
+        lax.fori_loop(0, valid[slot], finish_recv, 0)
+
+    for slot in range(slots):
+
         def finish_send(slot=slot):
             each(0, owners, lambda target: out_copy(slot, target, rank).wait_send())
 
+        def finish_land(source, carry, slot=slot):
+            land_copy(slot, source).wait()
+            return carry
+
         guarded(slot, rank, finish_send)
-
-        def finish_recv(source, carry, slot=slot):
-            out_copy(slot, rank, source).wait_recv()
-            return carry
-
-        lax.fori_loop(0, valid[slot], finish_recv, 0)
+        lax.fori_loop(0, valid[slot], finish_land, 0)
 
 
 def local(sections, owners, projected, gate, head_class, tile_lists, tile_counts):
@@ -270,7 +298,11 @@
         + [pltpu.VMEM((2, ntiles, tile_len, HD), jnp.bfloat16)] * slots
         + [pltpu.VMEM((tokens, HD), jnp.bfloat16)] * slots
         + [
+            pltpu.VMEM((slots * owners, 3, local_len // tile_len, tile_len, HD), jnp.bfloat16),
+            pltpu.VMEM((slots * owners, local_len, HD), jnp.bfloat16),
             pltpu.SemaphoreType.DMA((slots, 2)),
+            pltpu.SemaphoreType.DMA((slots, owners)),
+            pltpu.SemaphoreType.DMA((slots, owners)),
             pltpu.SemaphoreType.DMA((slots, owners)),
             pltpu.SemaphoreType.DMA((slots, owners)),
             pltpu.SemaphoreType.DMA((slots, owners)),

time: 161 us -> 162 us (level)
  no operation moved by 1% of the time
where the time goes in v5:
time: 162 us
  Pallas kernels  158 us (98%)
  local copies, waits for them, and re-layouts  3.76 us (2%)
    pallas_call x1, Pallas kernels, local(): pl.pallas_call(functools.partial(relay_kernel, heads, owners, sections, s...  158 us
    unnamed x1, local copies, waits for them, and re-layouts  3.76 us

profile of v5, /device:TPU:0, one launch (start us, length us, event | category | flops | bytes accessed | tf_op | source)
XLA Modules:
  0.0 161.7 jit_solution(563344137104440800)
XLA Ops:
  0.0 157.9 %shard_map.55 = bf16[512,3072]{1,0:T(8,128)(2,1)} custom-call(s32[24]{0:T(128)} %class_ref.1, s32[2,8,32]{2,1,0:T(8,128)} %bitcast.5, s32[24,32]{1,0:T(8,128)} %counts_ref.1, bf16[1,3072]{1,0:T(2,128)(2,1)} %gate_ref.1, bf16[3,4,128,3072]{3,2,1,0:T(8,128)(2,1)} %bitcast.4), custom_call_target="tpu_custom_call" | custom-call | flops 6442450944 | bytes 12582912 | tf_op jit(solution)/shard_map/pallas_call | solution.py:292
  157.9 3.8 %copy.7 = bf16[1,512,3072]{2,1,0:T(8,128)(2,1)} copy(bf16[1,512,3072]{2,1,0:T(8,128)(2,1)} %bitcast.3) | data formatting | bytes 6291456
